TPU v7x, 512 devices: a whole 4x8x8 slice. The times are simulated.
512 devices in a mesh: section: 16 (over y, core), expert: 8 (over x, z_lo), dp: 4 (over z_hi).
Axes of the slice: x: 4, y: 8, z: 8 (z_hi: 4, z_lo: 2; z = z_hi * 2 + z_lo), core: 2. Of those that a mesh axis runs over, the one named last changes fastest.
Arguments:
- x_fwd: bfloat16 [16, 2048, 3584], P('section', ('expert', 'dp')), may hold values from -6 to 6
- gain: float32 [16, 3584], P('section'), may hold values from 0.5 to 1.5
- w_up: bfloat16 [16, 3584, 4096], P('section', None, ('expert', 'dp')), may hold values from -0.09375 to 0.09375
- w_down: bfloat16 [16, 4096, 3584], P('section', ('expert', 'dp')), may hold values from -0.1875 to 0.1875
- routes_f: int32 [16, 2048, 2], P('section', ('expert', 'dp')), may hold values from 0 to 3, all different within a row; in each aligned block of 64 rows (0 to 63, 64 to 127, ..., all dimensions but the last counted through in order) at most 36 rows name the same one
- probs_f: float32 [16, 2048, 2], P('section', ('expert', 'dp')), may hold values from 0.2 to 1
- act_b: bfloat16 [16, 2048, 3584], P('section', ('expert', 'dp')), may hold values from -6 to 6
- grad_b: bfloat16 [16, 2048, 3584], P('section', ('expert', 'dp')), may hold values from -6 to 6
- routes_b: int32 [16, 2048, 2], P('section', ('expert', 'dp')), may hold values from 0 to 3, all different within a row; in each aligned block of 64 rows (0 to 63, 64 to 127, ..., all dimensions but the last counted through in order) at most 36 rows name the same one
- probs_b: float32 [16, 2048, 2], P('section', ('expert', 'dp')), may hold values from 0.2 to 1
Outputs:
- next_act: bfloat16 [16, 2048, 3584], P('section', ('expert', 'dp'))
- next_grad: bfloat16 [16, 2048, 3584], P('section', ('expert', 'dp'))
- gain_grad: float32 [16, 3584], P('section')
Inputs may be any that keep to these rules, and one draw needn't show every extreme that they name: `routes_f`: the 2 experts of a row differ. In each aligned block of 64 rows (the rows of one device) no expert is named by more than 36 picks, a bound that some block reaches. `routes_b`: the 2 experts of a row differ. In each aligned block of 64 rows (the rows of one device) no expert is named by more than 36 picks, a bound that some block reaches.
All inputs are finite; a program needn't handle non-finite values.
Results may differ from a plain program's by a relative error of at most 0.0053.
Values may be sent and summed in bfloat16 or wider, within the bound.
A program may use at most 128 MiB of HBM per device.

v0:
```python
import jax
import jax.numpy as jnp
from jax import lax
from jax.sharding import PartitionSpec as P

EXPERTS = 4
MOST = 36


EPS = 1e-06


def shifted(block, axis, distance):
    devices = range(lax.axis_size(axis))
    route = [((i - distance) % len(devices), i) for i in devices]
    return lax.ppermute(block, axis, route)


def apply_norm(rows, gain_gradient_row):
    wide_hidden = rows.astype(jnp.float32)
    inverse_scale = lax.rsqrt(jnp.mean(wide_hidden * wide_hidden, axis=-1, keepdims=True) + EPS)
    unit_rows = wide_hidden * inverse_scale
    return (unit_rows, inverse_scale, (unit_rows * gain_gradient_row).astype(jnp.bfloat16))


def slot_layout(routes, experts):
    picks = routes.reshape(-1)
    onehot = (picks[:, None] == jnp.arange(experts, dtype=jnp.int32)[None, :]).astype(jnp.int32)
    before = jnp.cumsum(onehot, axis=0) - onehot
    slots = jnp.sum(before * onehot, axis=1)
    return (picks, slots)


def fill_buffer(rows, picks, slots, experts, capacity):
    top = picks.shape[0] // rows.shape[0]
    source = jnp.repeat(rows, top, axis=0)
    return jnp.zeros((experts, capacity, rows.shape[1]), rows.dtype).at[picks, slots].set(source)


def pack(rows, picks, slots, experts, capacity, copies):
    buffer = fill_buffer(rows, picks, slots, experts, capacity)
    return jnp.repeat(buffer, copies, axis=0)


def unpack(back, picks, slots, probs, capacity, hosted, copies):
    count, depth, width = back.shape
    grouped = back.reshape(count // copies, copies, depth, width)
    picked = grouped[picks // hosted, :, picks % hosted * capacity + slots]
    summed = jnp.sum(picked.astype(jnp.float32), axis=1)
    weighted = summed * probs.reshape(-1)[:, None]
    tokens = probs.shape[0]
    return jnp.sum(weighted.reshape(tokens, -1, width), axis=1)


def expert_forward(received, slab_up, slab_down, hosted):
    count, depth, width = received.shape
    rows = received.reshape(count, hosted, depth // hosted, width)
    up_blocks = slab_up.reshape(width, hosted, -1)
    down_weight_blocks = slab_down.reshape(hosted, -1, width)
    pre = jnp.einsum("smcd,dmh->smch", rows, up_blocks, preferred_element_type=jnp.float32)
    hidden_state = jax.nn.silu(pre).astype(jnp.bfloat16)
    layer_output = jnp.einsum(
        "yoka,oan->yokn", hidden_state, down_weight_blocks, preferred_element_type=jnp.float32
    )
    return layer_output.astype(jnp.bfloat16).reshape(count, depth, width)


def expert_backward(received, received_grad, slab_up, slab_down, hosted):
    count, depth, width = received.shape
    rows = received.reshape(count, hosted, depth // hosted, width)
    gradient_list = received_grad.reshape(count, hosted, depth // hosted, width)
    up_blocks = slab_up.reshape(width, hosted, -1)
    down_weight_blocks = slab_down.reshape(hosted, -1, width)
    pre = jnp.einsum("smcd,dmh->smch", rows, up_blocks, preferred_element_type=jnp.float32)
    hidden_gradient = jnp.einsum(
        "eoip,obp->eoib", gradient_list, down_weight_blocks, preferred_element_type=jnp.float32
    )
    sig = jax.nn.sigmoid(pre)
    dpre = (hidden_gradient * sig * (1.0 + pre * (1.0 - sig))).astype(jnp.bfloat16)
    dn = jnp.einsum("smch,dmh->smcd", dpre, up_blocks, preferred_element_type=jnp.float32)
    return dn.astype(jnp.bfloat16).reshape(count, depth, width)


def body(x_fwd, gain, w_up, w_down, routes_f, probs_f, act_b, grad_b, routes_b, probs_b):
    ranks = lax.axis_size("expert")
    hosted = max(1, EXPERTS // ranks)
    copies = max(1, ranks // EXPERTS)
    capacity = MOST
    slab_up, slab_down = (
        lax.all_gather(w_up[0], "dp", axis=1, tiled=True),
        lax.all_gather(w_down[0], "dp", axis=0, tiled=True),
    )
    gain_gradient_row = gain[0]
    input_rows = x_fwd[0]
    activation_back_rows = act_b[0]
    gradient_back_rows = grad_b[0]
    forward_unit_rows, forward_scale, normed_forward_rows = apply_norm(
        input_rows, gain_gradient_row
    )
    backward_unit_rows, backward_scale, normed_backward_rows = apply_norm(
        activation_back_rows, gain_gradient_row
    )
    picks_f, slots_f = slot_layout(routes_f[0], EXPERTS)
    picks_b, slots_b = slot_layout(routes_b[0], EXPERTS)
    send_f = pack(normed_forward_rows, picks_f, slots_f, EXPERTS, capacity, copies)
    send_b = pack(normed_backward_rows, picks_b, slots_b, EXPERTS, capacity, copies)
    send_g = pack(gradient_back_rows, picks_b, slots_b, EXPERTS, capacity, copies)

    def gather_back(back, picks, slots, probs):
        return unpack(back, picks, slots, probs, capacity, hosted, copies)

    recv_f = lax.all_to_all(send_f, "expert", split_axis=0, concat_axis=0, tiled=True)
    back_f = lax.all_to_all(
        expert_forward(recv_f, slab_up, slab_down, hosted),
        "expert",
        split_axis=0,
        concat_axis=0,
        tiled=True,
    )
    recv_b, recv_g = (
        lax.all_to_all(send_b, "expert", split_axis=0, concat_axis=0, tiled=True),
        lax.all_to_all(send_g, "expert", split_axis=0, concat_axis=0, tiled=True),
    )
    back_b = lax.all_to_all(
        expert_backward(recv_b, recv_g, slab_up, slab_down, hosted),
        "expert",
        split_axis=0,
        concat_axis=0,
        tiled=True,
    )
    mixed = gather_back(back_f, picks_f, slots_f, probs_f[0])
    result = (input_rows.astype(jnp.float32) + mixed).astype(jnp.bfloat16)
    gradient_list = gather_back(back_b, picks_b, slots_b, probs_b[0])
    gain_gradient_total = lax.psum(
        jnp.sum(gradient_list * backward_unit_rows, axis=0), ("expert", "dp")
    )
    scaled_rows = gradient_list * gain_gradient_row
    input_gradient = gradient_back_rows.astype(jnp.float32) + backward_scale * (
        scaled_rows
        - backward_unit_rows * jnp.mean(scaled_rows * backward_unit_rows, axis=-1, keepdims=True)
    )
    next_act = shifted(result, "section", 1)
    next_grad = shifted(input_gradient.astype(jnp.bfloat16), "section", -1)
    return (next_act[None], next_grad[None], gain_gradient_total[None])


def solution(mesh):
    return jax.shard_map(
        body,
        mesh=mesh,
        in_specs=(
            P("section", ("expert", "dp"), None),
            P("section", None),
            P("section", None, ("expert", "dp")),
            P("section", ("expert", "dp"), None),
            P("section", ("expert", "dp"), None),
            P("section", ("expert", "dp"), None),
            P("section", ("expert", "dp"), None),
            P("section", ("expert", "dp"), None),
            P("section", ("expert", "dp"), None),
            P("section", ("expert", "dp"), None),
        ),
        out_specs=(
            P("section", ("expert", "dp"), None),
            P("section", ("expert", "dp"), None),
            P("section", None),
        ),
        check_vma=False,
    )
```

profile of v0, /device:TPU:56, one launch (start us, length us, event | category | flops | bytes accessed | tf_op | source)
XLA Modules:
  0.0 536.2 jit_solution(14403491271000730586)
XLA Ops:
  7.2 0.7 all-gather.5.cloned.1.call-update
  7.9 0.8 copy.48
  8.7 0.1 eq.37
  8.8 0.1 reshape_squeeze.7
  8.9 0.8 reduce
  9.7 1.2 fusion.40
  10.9 1.2 fusion.41
  12.2 1.2 fusion.33
  13.4 0.5 broadcast_in_dim.23
  13.8 0.3 reshape.268
  14.3 0.2 reduce_window_sum.18
  14.5 0.2 select_reduce_fusion
  14.6 0.3 broadcast.220.clone.1
  14.9 17.1 %scatter_fusion.2 = bf16[4,36,3584]{2,0,1:T(4,128)(2,1)S(1)} fusion(bf16[4,36,3584]{2,0,1:T(4,128)(2,1)S(1)} %broadcast.220.clone.1, s32[128]{0:T(128)S(1)} %get-tuple-element.5, bf16[128,3584]{1,0:T(8,128)(2,1)S(1)} %reshape.268), kind=kCustom, calls=%fused_computation.4 | custom fusion | bytes 2753536 | tf_op jit(solution)/shard_map/scatter | solution.py:37
  32.0 0.2 copy.51
  32.2 1.5 broadcast_in_dim.48
  33.7 6.2 %all-to-all-start.3 = ((bf16[8,36,3584]{2,1,0:T(8,128)(2,1)}), bf16[8,36,3584]{2,1,0:T(8,128)(2,1)}, u32[]{:S(2)}, u32[]{:S(2)}) async-start(bf16[8,36,3584]{2,1,0:T(8,128)(2,1)} %bitcast.28), calls=%async_computation.3 | async-start | bytes 4587520 | tf_op jit(solution)/shard_map/all_to_all | solution.py:121
  40.0 0.7 all-gather.7.cloned.1.call-update
  40.7 0.5 broadcast_in_dim.21
  41.2 0.3 reshape.262
  41.6 0.3 broadcast.220.clone
  41.8 17.1 %scatter_fusion.1 = bf16[4,36,3584]{2,0,1:T(4,128)(2,1)S(1)} fusion(bf16[4,36,3584]{2,0,1:T(4,128)(2,1)S(1)} %broadcast.220.clone, s32[128]{0:T(128)S(1)} %get-tuple-element.5, bf16[128,3584]{1,0:T(8,128)(2,1)S(1)} %reshape.262), kind=kCustom, calls=%fused_computation.3 | custom fusion | bytes 2753536 | tf_op jit(solution)/shard_map/scatter | solution.py:37
  58.9 0.2 copy.50
  59.1 55.7 %all-to-all-done.3 = bf16[8,36,3584]{2,1,0:T(8,128)(2,1)} async-done(((bf16[8,36,3584]{2,1,0:T(8,128)(2,1)}), bf16[8,36,3584]{2,1,0:T(8,128)(2,1)}, u32[]{:S(2)}, u32[]{:S(2)}) %all-to-all-start.3) | async-done | bytes 2064416 | tf_op jit(solution)/shard_map/all_to_all | solution.py:121
  114.7 1.5 broadcast_in_dim.22
  116.3 3.6 all-to-all-start.2
  119.9 5.0 fusion.11
  124.9 49.2 %all-to-all-done.2 = bf16[8,36,3584]{2,1,0:T(8,128)(2,1)S(1)} async-done(((bf16[8,36,3584]{2,1,0:T(8,128)(2,1)}), bf16[8,36,3584]{2,1,0:T(8,128)(2,1)S(1)}, u32[]{:S(2)}, u32[]{:S(2)}) %all-to-all-start.2) | async-done | bytes 2064416 | tf_op jit(solution)/shard_map/all_to_all | solution.py:122
  174.1 36.6 %all-gather.7.cloned.1.call-done = bf16[1,512,3584]{2,1,0:T(8,128)(2,1)} async-done(((bf16[1,128,3584]{2,1,0:T(8,128)(2,1)}), bf16[1,512,3584]{2,1,0:T(8,128)(2,1)}) %all-gather.7.cloned.1.call-update) | async-done | bytes 3670032 | tf_op jit(solution)/shard_map/all_gather | solution.py:91
  210.8 7.6 %convolution_convert_fusion = bf16[8,36,3584]{2,1,0:T(8,128)(2,1)} fusion(bf16[1,3584,512]{2,1,0:T(8,128)(2,1)} %all-gather.5.cloned.1.call-done, bf16[8,36,3584]{2,1,0:T(8,128)(2,1)S(1)} %all-to-all-done.2, bf16[1,512,3584]{2,1,0:T(8,128)(2,1)} %all-gather.7.cloned.1.call-done, f32[8,1,36,512]{3,2,0,1:T(8,128)} %fusion.11), kind=kOutput, calls=%fused_computation.5 | convolution fusion | flops 2116288512 | bytes 12058624 | tf_op jit(solution)/shard_map/smch,dmh->smcd/dot_general | solution.py:80
  218.4 4.9 all-to-all-start.4
  223.2 0.1 copy.42
  223.3 0.1 eq.33
  223.5 0.1 reshape_squeeze.6
  223.6 0.1 copy.53
  223.8 0.2 reduce_window_sum.17
  224.0 0.2 select_reduce_fusion.1
  224.2 28.3 %all-to-all-done.4 = bf16[8,36,3584]{2,1,0:T(8,128)(2,1)S(1)} async-done(((bf16[8,36,3584]{2,1,0:T(8,128)(2,1)}), bf16[8,36,3584]{2,1,0:T(8,128)(2,1)S(1)}, u32[]{:S(2)}, u32[]{:S(2)}) %all-to-all-start.4) | async-done | bytes 2064416 | tf_op jit(solution)/shard_map/all_to_all | solution.py:124
  252.5 3.0 copy.52
  255.4 6.0 %gather_fusion.1 = bf16[128,2,3584]{2,1,0:T(2,128)(2,1)S(1)} fusion(bf16[4,2,36,3584]{3,1,2,0:T(2,128)(2,1)} %copy.52, s32[128]{0:T(128)S(1)} %bitcast.127), kind=kCustom, calls=%fused_computation.1 | custom fusion | bytes 3671040 | tf_op jit(solution)/shard_map/gather | solution.py:48
  261.4 6.4 %convert_reduce_fusion = f32[128,3584]{1,0:T(8,128)} fusion(bf16[128,2,3584]{2,1,0:T(2,128)(2,1)S(1)} %gather_fusion.1), kind=kLoop, calls=%fused_computation.15 | loop fusion | flops 1376256 | bytes 3670016 | tf_op jit(solution)/shard_map/reduce_sum | solution.py:49
  267.9 2.6 reduce_sum.108
  270.5 2.6 multiply_reduce_fusion
  273.1 0.4 fusion.39
  273.5 1.2 fusion.38
  274.7 0.5 broadcast_in_dim.18
  275.2 0.3 reshape.256
  275.5 0.3 broadcast.220
  275.8 17.0 %scatter_fusion = bf16[4,36,3584]{2,0,1:T(4,128)(2,1)S(1)} fusion(bf16[4,36,3584]{2,0,1:T(4,128)(2,1)S(1)} %broadcast.220, s32[128]{0:T(128)S(1)} %get-tuple-element.7, bf16[128,3584]{1,0:T(8,128)(2,1)S(1)} %reshape.256), kind=kCustom, calls=%fused_computation.2 | custom fusion | bytes 2753536 | tf_op jit(solution)/shard_map/scatter | solution.py:37
  292.9 0.2 copy.44
  293.0 0.2 broadcast_in_dim.19
  293.2 32.1 %all_to_all.25 = bf16[8,36,3584]{2,1,0:T(8,128)(2,1)S(1)} all-to-all(bf16[8,36,3584]{2,1,0:T(8,128)(2,1)S(1)} %bitcast.126), channel_id=1, replica_groups=mesh['section'=16,'expert'=8,'dp'=4] {'expert'}, dimensions={0} | all-to-all | bytes 4128768 | tf_op jit(solution)/shard_map/all_to_all | solution.py:112
  325.3 7.4 %convolution_convert_fusion.1 = bf16[8,36,3584]{2,1,0:T(8,128)(2,1)} fusion(bf16[1,512,3584]{2,1,0:T(8,128)(2,1)} %all-gather.7.cloned.1.call-done, bf16[8,36,3584]{2,1,0:T(8,128)(2,1)S(1)} %all_to_all.25, bf16[1,3584,512]{2,1,0:T(8,128)(2,1)} %all-gather.5.cloned.1.call-done), kind=kOutput, calls=%fused_computation.6 | convolution fusion | flops 2115698688 | bytes 11468800 | tf_op jit(solution)/shard_map/yoka,oan->yokn/dot_general | solution.py:62
  332.6 4.1 all-to-all-start.1
  336.9 28.1 %all-to-all-done.1 = bf16[8,36,3584]{2,1,0:T(8,128)(2,1)S(1)} async-done(((bf16[8,36,3584]{2,1,0:T(8,128)(2,1)}), bf16[8,36,3584]{2,1,0:T(8,128)(2,1)S(1)}, u32[]{:S(2)}, u32[]{:S(2)}) %all-to-all-start.1) | async-done | bytes 2064416 | tf_op jit(solution)/shard_map/all_to_all | solution.py:113
  365.0 2.9 copy.45
  368.0 6.0 %gather_fusion = bf16[128,2,3584]{2,1,0:T(2,128)(2,1)S(1)} fusion(bf16[4,2,36,3584]{3,1,2,0:T(2,128)(2,1)} %copy.45, s32[128]{0:T(128)S(1)} %bitcast.128), kind=kCustom, calls=%fused_computation | custom fusion | bytes 3671040 | tf_op jit(solution)/shard_map/gather | solution.py:48
  374.0 6.3 %convert_reduce_fusion.1 = f32[128,3584]{1,0:T(8,128)} fusion(bf16[128,2,3584]{2,1,0:T(2,128)(2,1)S(1)} %gather_fusion), kind=kLoop, calls=%fused_computation.16 | loop fusion | flops 1376256 | bytes 3670016 | tf_op jit(solution)/shard_map/reduce_sum | solution.py:49
  380.3 2.6 reduce_sum.102
  382.9 2.5 multiply_reduce_fusion.1
  385.4 0.1 fusion.44
  385.6 141.0 %psum.7 = f32[1,3584]{1,0:T(1,128)} all-reduce(f32[1,3584]{1,0:T(1,128)S(1)} %broadcast_in_dim.50), channel_id=1, replica_groups=mesh['section'=16,'expert'=8,'dp'=4] {'expert','dp'}, use_global_device_ids=true, to_apply=%region_15.16 | all-reduce | flops 3584 | bytes 28672 | tf_op jit(solution)/shard_map/psum | solution.py:134
  526.6 0.8 copy.62
  527.4 1.8 copy.63
  (29 shorter events, 0.5 us)
Async XLA Ops:
  7.2 112.8 %all-gather.5.cloned.1.call-start = ((), (), s32[]{:S(2)}) async-start(), calls=%async_computation.5 | async-start | bytes 4587520 | tf_op jit(solution)/shard_map/all_gather | solution.py:90
  33.7 7.0 %copy-start.2 = (bf16[1,64,3584]{2,1,0:T(8,128)(2,1)S(1)}, bf16[1,64,3584]{2,1,0:T(8,128)(2,1)}, u32[]{:S(2)}) copy-start(bf16[1,64,3584]{2,1,0:T(8,128)(2,1)} %param.17) | copy-start | bytes 1376260
  33.7 81.0 %all-to-all-start.3 = ((bf16[8,36,3584]{2,1,0:T(8,128)(2,1)}), bf16[8,36,3584]{2,1,0:T(8,128)(2,1)}, u32[]{:S(2)}, u32[]{:S(2)}) async-start(bf16[8,36,3584]{2,1,0:T(8,128)(2,1)} %bitcast.28), calls=%async_computation.3 | async-start | bytes 4587520 | tf_op jit(solution)/shard_map/all_to_all | solution.py:121
  40.0 170.8 %all-gather.7.cloned.1.call-start = ((), (), s32[]{:S(2)}) async-start(), calls=%async_computation.6 | async-start | bytes 4587520 | tf_op jit(solution)/shard_map/all_gather | solution.py:91
  116.3 57.8 %all-to-all-start.2 = ((bf16[8,36,3584]{2,1,0:T(8,128)(2,1)}), bf16[8,36,3584]{2,1,0:T(8,128)(2,1)S(1)}, u32[]{:S(2)}, u32[]{:S(2)}) async-start(bf16[8,36,3584]{2,1,0:T(8,128)(2,1)} %bitcast.23), calls=%async_computation.2 | async-start | bytes 4587520 | tf_op jit(solution)/shard_map/all_to_all | solution.py:122
  218.4 4.9 copy-start.4
  218.4 5.3 copy-start.5
  218.4 34.1 %all-to-all-start.4 = ((bf16[8,36,3584]{2,1,0:T(8,128)(2,1)}), bf16[8,36,3584]{2,1,0:T(8,128)(2,1)S(1)}, u32[]{:S(2)}, u32[]{:S(2)}) async-start(bf16[8,36,3584]{2,1,0:T(8,128)(2,1)} %convolution_convert_fusion), calls=%async_computation.4 | async-start | bytes 4587520 | tf_op jit(solution)/shard_map/all_to_all | solution.py:124
  270.5 2.6 copy-start
  270.5 3.0 copy-start.1
  332.6 4.2 copy-start.6
  332.6 4.3 copy-start.3
  332.6 32.4 %all-to-all-start.1 = ((bf16[8,36,3584]{2,1,0:T(8,128)(2,1)}), bf16[8,36,3584]{2,1,0:T(8,128)(2,1)S(1)}, u32[]{:S(2)}, u32[]{:S(2)}) async-start(bf16[8,36,3584]{2,1,0:T(8,128)(2,1)} %convolution_convert_fusion.1), calls=%async_computation.1 | async-start | bytes 4587520 | tf_op jit(solution)/shard_map/all_to_all | solution.py:113
  336.9 189.7 %collective-permute-start.1 = (bf16[64,3584]{1,0:T(8,128)(2,1)S(1)}, bf16[64,3584]{1,0:T(8,128)(2,1)}, u32[]{:S(2)}, u32[]{:S(2)}) collective-permute-start(bf16[64,3584]{1,0:T(8,128)(2,1)S(1)} %copy-done.3), channel_id=1, source_target_pairs={{32,0},{64,32},{96,64},{128,96},{160,128},{192,160},{224,192},{256... | collective-permute-start | bytes 1376264 | tf_op jit(solution)/shard_map/ppermute | solution.py:16
  385.5 141.1 %collective-permute-start = (bf16[64,3584]{1,0:T(8,128)(2,1)S(1)}, bf16[64,3584]{1,0:T(8,128)(2,1)S(1)}, u32[]{:S(2)}, u32[]{:S(2)}) collective-permute-start(bf16[64,3584]{1,0:T(8,128)(2,1)S(1)} %fusion.44), channel_id=1, source_target_pairs={{480,0},{0,32},{32,64},{64,96},{96,128},{128,160},{160,192},{192,2... | collective-permute-start | bytes 1376264 | tf_op jit(solution)/shard_map/ppermute | solution.py:16
Sparse Core Ops, SparseCore 0:
  10.1 109.1 all-gather.4
  121.4 89.3 all-gather.6
where the time goes:
time: 545 us; the launch traced here: 536 us
  waiting for transfers between devices  199 us (37%)
  blocking collectives  173 us (32%)
  local copies, waits for them, and re-layouts  85.5 us (16%)
  other arithmetic  24.8 us (5%)
  matrix products  19.9 us (4%)
  starting transfers between devices  19 us (3%)
  between operations  14.6 us (3%)
    psum x1, blocking collectives, body(): lax.psum(jnp.sum(gradient_list * backward_unit_rows, axis=0), ('expert',...  141 us
    all_to_all x1, waiting for transfers between devices, body(): lax.all_to_all(send_b, 'expert', split_axis=0, concat_axis=0, tiled=True)  55.7 us
    scatter x6, local copies, waits for them, and re-layouts, fill_buffer(): jnp.zeros((experts, capacity, rows.shape[1]), rows.dtype).at[picks, slots]  51.7 us
    all_to_all x1, waiting for transfers between devices, body(): lax.all_to_all(send_g, 'expert', split_axis=0, concat_axis=0, tiled=True)  49.2 us
    all_gather x1, waiting for transfers between devices, body(): lax.all_gather(w_down[0], 'dp', axis=0, tiled=True)  36.6 us
    all_to_all x1, blocking collectives, body(): lax.all_to_all(send_f, 'expert', split_axis=0, concat_axis=0, tiled=True)  32.1 us
    all_to_all x1, waiting for transfers between devices, body(): lax.all_to_all(expert_backward(recv_b, recv_g, slab_up, slab_down, hosted...  28.3 us
    all_to_all x1, waiting for transfers between devices, body(): lax.all_to_all(expert_forward(recv_f, slab_up, slab_down, hosted), 'exper...  28.1 us
  transfers between devices with their start and end apart: 8, of which 5 were waited for; matrix products, arithmetic and copies ran while one was open for 13% of the time, Pallas kernels for 0%

commit v1 on v0

v1 whole, which is shorter than its diff:
```python
import functools

import jax
import jax.numpy as jnp
from jax import lax
from jax.experimental import pallas as pl
from jax.experimental.pallas import tpu as pltpu
from jax.sharding import PartitionSpec as P

EXPERTS = 4
MOST = 36
EPS = 1e-06
ROWS = 48
CHUNKS = 4
LANES = 256
TOKEN_STEP = 3
MESH = pl.DeviceIdType.MESH
F32 = jnp.float32
BF16 = jnp.bfloat16


def nt(a, b):
    return lax.dot_general(a, b, (((1,), (1,)), ((), ())), preferred_element_type=F32)


def tn(a, b):
    return lax.dot_general(a, b, (((0,), (0,)), ((), ())), preferred_element_type=F32)


def nn(a, b):
    return jnp.dot(a, b, preferred_element_type=F32)


def relay(
    dims,
    x_ref, gain_ref, up_in, down_in, rf_ref, pf_ref, act_ref, g_ref, rb_ref, pb_ref,
    act_out, grad_out, gain_out,
    up, down, packs, tok_n, tok_g, pre, hid, dh, out_acc, ret_f, ret_b, back_f, back_b,
    x_in, act_in, g_in, gain_in, wf, wb, wf_in, wb_in, qg, gpart, gx, gz_own, gz,
    z_send, z_recv, own_sem, t_send, t_recv, f_send, f_recv, b_send, b_recv,
    s_send, s_recv, gx_send, gx_recv, gz_send, gz_recv,
):
    sections, nz, zlo = dims
    tokens, width = x_ref.shape
    wide = width // CHUNKS
    used = EXPERTS * ROWS
    s, e, d = lax.axis_index("section"), lax.axis_index("expert"), lax.axis_index("dp")
    x, z = e // zlo, d * zlo + e % zlo
    nxt, prv = lax.rem(s + 1, sections), lax.rem(s + sections - 1, sections)
    sign = 1 - 2 * lax.rem(s, 2)
    reach_a, reach_b = nz // 2, nz // 2 - 1

    def place(section, xx, zz):
        return (section, xx * zlo + lax.rem(zz, zlo), zz // zlo)

    def at_x(k):
        return lax.rem(x + k + EXPERTS, EXPERTS)

    def at_z(k):
        return lax.rem(z + k + nz, nz)

    peers = [place(s, at_x(k), z) for k in range(1, EXPERTS)]
    peers += [place(s, x, at_z(k)) for k in range(1, nz)]
    peers += [place(nxt, at_x(k), z) for k in range(EXPERTS)]
    peers += [place(prv, at_x(k), z) for k in range(EXPERTS)]
    barrier = pltpu.get_barrier_semaphore()
    for peer in peers:
        pl.semaphore_signal(barrier, inc=1, device_id=peer, device_id_type=MESH)
    pl.semaphore_wait(barrier, len(peers))

    sent = []

    def send(src, dst, send_sem, recv_sem, device):
        copy = pltpu.make_async_remote_copy(
            src_ref=src, dst_ref=dst, send_sem=send_sem, recv_sem=recv_sem,
            device_id=device, device_id_type=MESH,
        )
        copy.start()
        sent.append(copy)
        return copy

    long_way, short_way = place(s, x, at_z(sign)), place(s, x, at_z(-sign))
    moving = {}

    def own_piece(c):
        if c < CHUNKS:
            return up_in.at[c]
        return down_in.at[:, pl.ds((c - CHUNKS) * wide, wide)]

    def held(slot, c):
        return up.at[slot, c] if c < CHUNKS else down.at[slot, c - CHUNKS]

    def pass_on(c, frm, to, device):
        src = own_piece(c) if frm == 0 else held(frm, c)
        moving[c, to] = send(
            src, held(to, c), z_send.at[c, to - 1], z_recv.at[c, to - 1], device
        )

    def start_own(c):
        pass_on(c, 0, 1, long_way)
        pass_on(c, 0, reach_a + 1, short_way)

    def pass_round(c, r):
        moving[c, r].wait_recv()
        if r < reach_a:
            pass_on(c, r, r + 1, long_way)
        if r <= reach_b:
            moving[c, reach_a + r].wait_recv()
            if r < reach_b:
                pass_on(c, reach_a + r, reach_a + r + 1, short_way)

    start_own(0)
    start_own(1)
    start_own(2)
    keep = [pltpu.make_async_copy(own_piece(c), held(0, c), own_sem.at[c]) for c in range(2 * CHUNKS)]
    for copy in keep:
        copy.start()

    ahead, behind = place(nxt, x, z), place(prv, x, z)
    arriving = {}
    arriving["x"] = send(x_ref, x_in, s_send.at[0], s_recv.at[0], ahead)
    arriving["act"] = send(act_ref, act_in, s_send.at[1], s_recv.at[1], behind)
    arriving["g"] = send(g_ref, g_in, s_send.at[2], s_recv.at[2], behind)
    arriving["gain"] = send(gain_ref, gain_in, s_send.at[3], s_recv.at[3], behind)

    column = lax.broadcasted_iota(jnp.int32, (tokens, LANES), 1)
    block = sum((column >= k * ROWS).astype(jnp.int32) for k in range(1, EXPERTS))
    slot = (column - block * ROWS).astype(F32)
    expert = x + block
    expert = jnp.where(expert >= EXPERTS, expert - EXPERTS, expert)
    earlier = (
        lax.broadcasted_iota(jnp.int32, (tokens, tokens), 1)
        < lax.broadcasted_iota(jnp.int32, (tokens, tokens), 0)
    ).astype(F32).astype(BF16)

    def layout(r_ref, p_ref):
        first, second = r_ref[:, 0:1] == expert, r_ref[:, 1:2] == expert
        chosen = jnp.where(first | second, 1.0, 0.0)
        before = nn(earlier, chosen.astype(BF16))
        taken = (before == slot) & (chosen > 0.5) & (column < used)
        weight = jnp.where(first, p_ref[:, 0:1], 0.0) + jnp.where(second, p_ref[:, 1:2], 0.0)
        return jnp.where(taken, 1.0, 0.0).astype(BF16)[:, :used], jnp.where(taken, weight, 0.0)

    pick_b, weight_b = layout(rb_ref, pb_ref)
    pick_f, weight_f = layout(rf_ref, pf_ref)
    wf[...] = weight_f
    wb[...] = weight_b
    arriving["wf"] = send(wf, wf_in, s_send.at[4], s_recv.at[4], ahead)
    arriving["wb"] = send(wb, wb_in, s_send.at[5], s_recv.at[5], behind)

    def part(ref, c):
        return ref[:, c * wide:(c + 1) * wide]

    def scale_of(ref):
        total = jnp.zeros((tokens, 1), F32)
        for c in range(CHUNKS):
            v = part(ref, c).astype(F32)
            total = total + jnp.sum(v * v, axis=-1, keepdims=True)
        return lax.rsqrt(total / width + EPS)

    def distribute(index, pick, rows_of, kept, base):
        for c in range(CHUNKS):
            rows = tn(pick, rows_of(c)).astype(BF16)
            packs[index, c] = rows
            kept[c, base:base + ROWS, :] = rows[:ROWS]
        for k in range(1, EXPERTS):
            n = index * (EXPERTS - 1) + k - 1
            arriving["tok", index, k] = send(
                packs.at[index, :, pl.ds(k * ROWS, ROWS), :],
                kept.at[:, pl.ds(base + k * ROWS, ROWS), :],
                t_send.at[n], t_recv.at[n], place(s, at_x(k), z),
            )

    def normed(ref):
        scale = scale_of(ref)
        return lambda c: (part(ref, c).astype(F32) * scale * part(gain_ref, c)).astype(BF16)

    distribute(0, pick_f, normed(x_ref), tok_n, 0)
    distribute(1, pick_b, normed(act_ref), tok_n, used)
    distribute(2, pick_b, lambda c: part(g_ref, c), tok_g, 0)
    for copy in keep:
        copy.wait()

    def tokens_of(index):
        for k in range(1, EXPERTS):
            arriving["tok", index, k].wait_recv()

    def both(ref, pair, c, axis):
        one, other = (0, reach_a) if pair == 0 else (pair, reach_a + pair)
        return jnp.concatenate([ref[one, c], ref[other, c]], axis=axis)

    def up_piece(c, pair, step):
        term = nn(tok_n[c], both(up, pair, c, 1))
        if c == 0:
            pre[pair] = term
        else:
            pre[pair] += term
        if c == CHUNKS - 1:
            v = pre[pair, :used, :]
            hid[pair] = (v * jax.nn.sigmoid(v)).astype(BF16)

    def down_piece(c, pair, step):
        block_of = both(down, pair, c, 0)
        term = nt(tok_g[c], block_of)
        if c == 0:
            dh[pair] = term
        else:
            dh[pair] += term
        term = nn(hid[pair], block_of)
        if pair == 1 % (nz // 2):
            out_acc[c] = term
        elif pair != 0:
            out_acc[c] += term
        else:
            ret_f[c] = (out_acc[c] + term).astype(BF16)
            give_back("f", c, ret_f, back_f, f_send, f_recv, nxt)

    def give_back(name, c, src, dst, send_sem, recv_sem, section):
        for k in range(EXPERTS):
            rows = pl.ds(k * ROWS, ROWS)
            arriving[name, c, k] = send(
                src.at[c, rows, :], dst.at[c, rows, :],
                send_sem.at[c, k], recv_sem.at[c, k], place(section, at_x(-k), z),
            )

    waiting = []
    have_n = have_g = False
    for t in range(1, 2 * CHUNKS + reach_a):
        if 3 <= t + 1 < 2 * CHUNKS:
            start_own(t + 1)
        for r in range(1, reach_a + 1):
            c = t - r
            if 0 <= c < 2 * CHUNKS:
                pass_round(c, r)
                waiting.append((c, r % reach_a))
        if t >= TOKEN_STEP:
            if not have_n:
                tokens_of(0)
                tokens_of(1)
                have_n = True
            for c, pair in waiting:
                if c < CHUNKS:
                    up_piece(c, pair, t)
                else:
                    if not have_g:
                        tokens_of(2)
                        have_g = True
                    down_piece(c - CHUNKS, pair, t)
            waiting = []

    dpre = []
    for pair in range(nz // 2):
        v = pre[pair, used:, :]
        sig = jax.nn.sigmoid(v)
        dpre.append((dh[pair] * sig * (1.0 + v * (1.0 - sig))).astype(BF16))
    for c in range(CHUNKS):
        total = nt(dpre[0], both(up, 0, c, 1))
        for pair in range(1, nz // 2):
            total = total + nt(dpre[pair], both(up, pair, c, 1))
        ret_b[c] = total.astype(BF16)
        give_back("b", c, ret_b, back_b, b_send, b_recv, prv)

    def gathered(weights, back, c):
        w = weights[:, :used]
        high = w.astype(BF16)
        low = (w - high.astype(F32)).astype(BF16)
        return nn(high, back[c]) + nn(low, back[c])

    arriving["x"].wait_recv()
    arriving["wf"].wait_recv()
    for c in range(CHUNKS):
        for k in range(EXPERTS):
            arriving["f", c, k].wait_recv()
        mixed = gathered(wf_in, back_f, c)
        act_out[:, c * wide:(c + 1) * wide] = (part(x_in, c).astype(F32) + mixed).astype(BF16)

    for name in ("act", "g", "gain", "wb"):
        arriving[name].wait_recv()
    scale = scale_of(act_in)
    dot = jnp.zeros((tokens, 1), F32)
    for c in range(CHUNKS):
        for k in range(EXPERTS):
            arriving["b", c, k].wait_recv()
        q = gathered(wb_in, back_b, c)
        xhat = part(act_in, c).astype(F32) * scale
        gpart[:, c * wide:(c + 1) * wide] = jnp.sum(q * xhat, axis=0, keepdims=True)
        scaled = q * part(gain_in, c)
        qg[c] = scaled
        dot = dot + jnp.sum(scaled * xhat, axis=-1, keepdims=True)
    for k in range(EXPERTS):
        arriving["gx", k] = send(
            gpart, gx.at[x], gx_send.at[k], gx_recv.at[x], place(nxt, at_x(k), z)
        )
    mean = dot / width
    for c in range(CHUNKS):
        xhat = part(act_in, c).astype(F32) * scale
        dx = part(g_in, c).astype(F32) + scale * (qg[c] - xhat * mean)
        grad_out[:, c * wide:(c + 1) * wide] = dx.astype(BF16)
    for k in range(EXPERTS):
        pltpu.make_async_remote_copy(
            src_ref=gpart, dst_ref=gx.at[k], send_sem=gx_send.at[k], recv_sem=gx_recv.at[k],
            device_id=ahead, device_id_type=MESH,
        ).wait_recv()
    total = gx[0]
    for k in range(1, EXPERTS):
        total = total + gx[k]
    gz_own[...] = total
    gz[z] = total
    for k in range(1, nz):
        send(gz_own, gz.at[z], gz_send.at[k - 1], gz_recv.at[z], place(s, x, at_z(k)))
    for k in range(1, nz):
        frm = at_z(k)
        pltpu.make_async_remote_copy(
            src_ref=gz_own, dst_ref=gz.at[frm], send_sem=gz_send.at[k - 1],
            recv_sem=gz_recv.at[frm], device_id=long_way, device_id_type=MESH,
        ).wait_recv()
    total = gz[0]
    for k in range(1, nz):
        total = total + gz[k]
    gain_out[...] = total
    for copy in sent:
        copy.wait_send()


def body(sections, ranks, dp, x_fwd, gain, w_up, w_down, routes_f, probs_f, act_b, grad_b, routes_b, probs_b):
    zlo = ranks // EXPERTS
    nz = zlo * dp
    tokens, width = x_fwd.shape[1:]
    wide = width // CHUNKS
    hidden = w_up.shape[-1]
    used = EXPERTS * ROWS
    pairs = nz // 2
    vmem, anywhere = pl.BlockSpec(memory_space=pltpu.VMEM), pl.BlockSpec(memory_space=pl.ANY)
    dma = pltpu.SemaphoreType.DMA
    scratch = [
        pltpu.VMEM((nz, CHUNKS, wide, hidden), BF16),
        pltpu.VMEM((nz, CHUNKS, hidden, wide), BF16),
        pltpu.VMEM((3, CHUNKS, used, wide), BF16),
        pltpu.VMEM((CHUNKS, 2 * used, wide), BF16),
        pltpu.VMEM((CHUNKS, used, wide), BF16),
        pltpu.VMEM((pairs, 2 * used, 2 * hidden), F32),
        pltpu.VMEM((pairs, used, 2 * hidden), BF16),
        pltpu.VMEM((pairs, used, 2 * hidden), F32),
        pltpu.VMEM((CHUNKS, used, wide), F32),
        pltpu.VMEM((CHUNKS, used, wide), BF16),
        pltpu.VMEM((CHUNKS, used, wide), BF16),
        pltpu.VMEM((CHUNKS, used, wide), BF16),
        pltpu.VMEM((CHUNKS, used, wide), BF16),
        pltpu.VMEM((tokens, width), BF16),
        pltpu.VMEM((tokens, width), BF16),
        pltpu.VMEM((tokens, width), BF16),
        pltpu.VMEM((1, width), F32),
        pltpu.VMEM((tokens, LANES), F32),
        pltpu.VMEM((tokens, LANES), F32),
        pltpu.VMEM((tokens, LANES), F32),
        pltpu.VMEM((tokens, LANES), F32),
        pltpu.VMEM((CHUNKS, tokens, wide), F32),
        pltpu.VMEM((1, width), F32),
        pltpu.VMEM((EXPERTS, 1, width), F32),
        pltpu.VMEM((1, width), F32),
        pltpu.VMEM((nz, 1, width), F32),
        dma((2 * CHUNKS, nz - 1)), dma((2 * CHUNKS, nz - 1)), dma((2 * CHUNKS,)),
        dma((3 * (EXPERTS - 1),)), dma((3 * (EXPERTS - 1),)),
        dma((CHUNKS, EXPERTS)), dma((CHUNKS, EXPERTS)),
        dma((CHUNKS, EXPERTS)), dma((CHUNKS, EXPERTS)),
        dma((6,)), dma((6,)),
        dma((EXPERTS,)), dma((EXPERTS,)), dma((nz - 1,)), dma((nz,)),
    ]
    act, grad, gain_grad = pl.pallas_call(
        functools.partial(relay, (sections, nz, zlo)),
        out_shape=(
            jax.ShapeDtypeStruct((tokens, width), BF16),
            jax.ShapeDtypeStruct((tokens, width), BF16),
            jax.ShapeDtypeStruct((1, width), F32),
        ),
        in_specs=[vmem, vmem, anywhere, anywhere] + [vmem] * 6,
        out_specs=(vmem, vmem, vmem),
        scratch_shapes=scratch,
        compiler_params=pltpu.CompilerParams(
            collective_id=0, has_side_effects=True, vmem_limit_bytes=52 * 2**20
        ),
    )(
        x_fwd[0], gain, w_up.reshape(CHUNKS, wide, hidden), w_down[0],
        routes_f[0], probs_f[0], act_b[0], grad_b[0], routes_b[0], probs_b[0],
    )
    return act[None], grad[None], gain_grad


def solution(mesh):
    sizes = mesh.shape
    rows, weights = P("section", ("expert", "dp"), None), P("section", None, ("expert", "dp"))
    return jax.shard_map(
        functools.partial(body, sizes["section"], sizes["expert"], sizes["dp"]),
        mesh=mesh,
        in_specs=(rows, P("section", None), weights) + (rows,) * 7,
        out_specs=(rows, rows, P("section", None)),
        check_vma=False,
    )
```

time: 545 us -> 197 us (0.36)
  waiting for transfers between devices: 199 us -> 0 us
  Pallas kernels: 0 us -> 185 us
  blocking collectives: 173 us -> 0 us
  local copies, waits for them, and re-layouts: 85.5 us -> 7.59 us
  other arithmetic: 24.8 us -> 0 us
  matrix products: 19.9 us -> 0 us
  starting transfers between devices: 19 us -> 0 us
  between operations: 14.6 us -> 0.66 us
    pallas_call x0 -> x1, Pallas kernels: none -> 185 us  [body(): pl.pallas_call(functools.partial(relay, (sections, nz, zlo)), out_shape=(...]
    all_to_all x4 -> x0, waiting for transfers between devices: 161 us -> none  [the longest x1 55.7 us: body(): lax.all_to_all(send_b, 'expert', split_axis=0, concat_axis=0, tiled=True)]
    psum x1 -> x0, blocking collectives: 141 us -> none  [body(): lax.psum(jnp.sum(gradient_list * backward_unit_rows, axis=0), ('expert',...]
    scatter x6 -> x0, local copies, waits for them, and re-layouts: 51.7 us -> none  [fill_buffer(): jnp.zeros((experts, capacity, rows.shape[1]), rows.dtype).at[picks, slots]]
    all_gather x2 -> x0, waiting for transfers between devices: 36.7 us -> none  [the longest x1 36.6 us: body(): lax.all_gather(w_down[0], 'dp', axis=0, tiled=True)]
    all_to_all x1 -> x0, blocking collectives: 32.1 us -> none  [body(): lax.all_to_all(send_f, 'expert', split_axis=0, concat_axis=0, tiled=True)]
    reduce_sum x9 -> x0, other arithmetic: 21 us -> none  [the longest x2 12.8 us: unpack(): summed = jnp.sum(picked.astype(jnp.float32), axis=1)]
    dot_general x3 -> x0, matrix products: 19.9 us -> none  [the longest x1 7.61 us: expert_backward(): jnp.einsum('smch,dmh->smcd', dpre, up_blocks, preferred_element_type=jnp....]
  transfers between devices with their start and end apart: 8 -> 0, of which waited for: 5 -> 0; matrix products, arithmetic and copies ran while one was open for 13% -> 0% of each run, Pallas kernels for 0% -> 0%
where the time goes in v1:
time: 197 us; the launch traced here: 193 us
  Pallas kernels  185 us (94%)
  local copies, waits for them, and re-layouts  7.59 us (4%)
    pallas_call x1, Pallas kernels, body(): pl.pallas_call(functools.partial(relay, (sections, nz, zlo)), out_shape=(...  185 us
    unnamed x17, local copies, waits for them, and re-layouts  7.21 us

profile of v1, /device:TPU:56, one launch (start us, length us, event | category | flops | bytes accessed | tf_op | source)
XLA Modules:
  0.0 193.4 jit_solution(9276434126464963192)
XLA Ops:
  0.6 0.0 copy-start.3
  0.6 0.7 copy-done.3
  1.3 0.0 copy-start.4
  1.3 0.1 copy.13.rf_ref
  1.4 0.6 copy-done.4
  2.0 0.0 copy-start.5
  2.0 0.1 copy.14.pf_ref
  2.1 0.6 copy-done.5
  2.7 0.0 copy-start.6
  2.7 0.1 copy.15.rb_ref
  2.8 0.6 copy-done.6
  3.3 0.0 copy-start.2
  3.4 0.1 copy.16.pb_ref
  3.4 0.6 copy-done.2
  4.1 0.0 copy-start
  4.1 1.0 copy-done
  5.1 0.0 copy-start.1
  5.1 1.0 copy-done.1
  6.1 185.2 %shard_map.121 = (bf16[64,3584]{1,0:T(8,128)(2,1)S(1)}, bf16[64,3584]{1,0:T(8,128)(2,1)S(1)}, f32[1,3584]{1,0:T(1,128)S(1)}) custom-call(bf16[64,3584]{1,0:T(8,128)(2,1)S(1)} %bitcast.13, f32[1,3584]{1,0:T(1,128)S(1)} %copy-done.2, bf16[4,896,128]{2,1,0:T(8,128)(2,1)} %bitcast.15, bf16[128,3584]{1,0:T(8,128)(2,1)} %bitcast.16, s32[64,2]{1,0:T(8,128)S(1)} %copy.13.rf_ref, ...), custom_call_target="tpu_custom_call" | custom-call | tf_op jit(solution)/shard_map/pallas_call | solution.py:369
  191.3 0.8 copy.20
  192.1 0.8 copy.21
  192.8 0.6 copy.22
Async XLA Ops:
  0.6 0.7 copy-start.3
  1.3 0.7 copy-start.4
  2.0 0.7 copy-start.5
  2.7 0.7 copy-start.6
  3.3 0.7 copy-start.2
  4.1 1.0 copy-start
  5.1 1.0 copy-start.1

commit v2 on v1

v2 whole, which is shorter than its diff:
```python
import functools

import jax
import jax.numpy as jnp
from jax import lax
from jax.experimental import pallas as pl
from jax.experimental.pallas import tpu as pltpu
from jax.sharding import PartitionSpec as P

EXPERTS = 4
EPS = 1e-06
MAIN = 32
REST = 4
SLOTS = EXPERTS * (MAIN + REST)
MAINS = EXPERTS * MAIN
LANE = 128
PIECE = LANE * MAIN // REST
FINE = PIECE // 2
TOKEN_STEP = 4
MESH = pl.DeviceIdType.MESH
F32 = jnp.float32
BF16 = jnp.bfloat16


def nt(a, b):
    return lax.dot_general(a, b, (((1,), (1,)), ((), ())), preferred_element_type=F32)


def tn(a, b):
    return lax.dot_general(a, b, (((0,), (0,)), ((), ())), preferred_element_type=F32)


def nn(a, b):
    return jnp.dot(a, b, preferred_element_type=F32)


def cuts(width, piece=PIECE):
    return [(at, min(piece, width - at)) for at in range(0, width, piece)]


def relay(
    dims,
    x_hbm, gain_hbm, up_in, down_in, rf_hbm, pf_hbm, act_hbm, g_hbm, rb_hbm, pb_hbm,
    act_out, grad_out, gain_out,
    x_ref, gain_ref, rf_ref, pf_ref, act_ref, g_ref, rb_ref, pb_ref,
    up, down, packs, tok, rest, pre, hid, dh, dpre, out_acc, dn_acc, ret_f, ret_b, back_f, back_b,
    x_in, act_in, g_in, gain_in, wf, wb, wf_in, wb_in, qg, gpart, gz, gx_own, gx,
    in_sem, own_sem, z_send, z_recv, t_send, t_recv, f_send, f_recv, b_send, b_recv,
    s_send, s_recv, gx_send, gx_recv, gz_send, gz_recv,
):
    sections, nz, zlo = dims
    tokens, width = x_ref.shape
    parts = cuts(width)
    pieces = len(parts)
    fine = cuts(width, FINE)
    fines = len(fine)
    all_cuts = parts + fine
    last = len(all_cuts)
    pairs = nz // 2
    s, e, d = lax.axis_index("section"), lax.axis_index("expert"), lax.axis_index("dp")
    x, z = e // zlo, d * zlo + e % zlo
    nxt, prv = lax.rem(s + 1, sections), lax.rem(s + sections - 1, sections)
    sign = 1 - 2 * lax.rem(s, 2)
    reach_a, reach_b = nz // 2, nz // 2 - 1

    def place(section, xx, zz):
        return (section, xx * zlo + lax.rem(zz, zlo), zz // zlo)

    def at_x(k):
        return lax.rem(x + k + EXPERTS, EXPERTS)

    def at_z(k):
        return lax.rem(z + k + nz, nz)

    peers = [place(s, x, at_z(k)) for k in range(1, nz)]
    peers += [place(s, at_x(k), z) for k in range(1, EXPERTS)]
    peers += [place(nxt, at_x(k), z) for k in range(EXPERTS)]
    peers += [place(prv, at_x(k), z) for k in range(EXPERTS)]
    barrier = pltpu.get_barrier_semaphore()
    for peer in peers:
        pl.semaphore_signal(barrier, inc=1, device_id=peer, device_id_type=MESH)
    fetched = [
        (rf_hbm, rf_ref), (rb_hbm, rb_ref), (pf_hbm, pf_ref), (pb_hbm, pb_ref), (gain_hbm, gain_ref),
        (x_hbm, x_ref), (act_hbm, act_ref), (g_hbm, g_ref),
    ]
    fetched = [pltpu.make_async_copy(a, b, in_sem.at[i]) for i, (a, b) in enumerate(fetched)]
    for copy in fetched:
        copy.start()
    pl.semaphore_wait(barrier, len(peers))

    sent = []

    def send(src, dst, send_sem, recv_sem, device):
        copy = pltpu.make_async_remote_copy(
            src_ref=src, dst_ref=dst, send_sem=send_sem, recv_sem=recv_sem,
            device_id=device, device_id_type=MESH,
        )
        copy.start()
        sent.append(copy)
        return copy

    long_way, short_way = place(s, x, at_z(sign)), place(s, x, at_z(-sign))
    moving = {}

    def own_piece(c):
        at, size = all_cuts[c]
        return up_in.at[pl.ds(at, size), :] if c < pieces else down_in.at[:, pl.ds(at, size)]

    def held(slot, c):
        at, size = all_cuts[c]
        return up.at[slot, pl.ds(at, size), :] if c < pieces else down.at[slot, :, pl.ds(at, size)]

    def pass_on(c, frm, to, device):
        src = own_piece(c) if frm == 0 else held(frm, c)
        moving[c, to] = send(
            src, held(to, c), z_send.at[c, to - 1], z_recv.at[c, to - 1], device
        )

    def start_own(c):
        pass_on(c, 0, 1, long_way)
        pass_on(c, 0, reach_a + 1, short_way)

    def pass_round(c, r):
        moving[c, r].wait_recv()
        if r < reach_a:
            pass_on(c, r, r + 1, long_way)
        if r <= reach_b:
            moving[c, reach_a + r].wait_recv()
            if r < reach_b:
                pass_on(c, reach_a + r, reach_a + r + 1, short_way)

    for c in range(3):
        start_own(c)
    keep = [pltpu.make_async_copy(up_in, up.at[0], own_sem.at[0]), pltpu.make_async_copy(down_in, down.at[0], own_sem.at[1])]
    for copy in keep:
        copy.start()
    for copy in fetched:
        copy.wait()

    ahead, behind = place(nxt, x, z), place(prv, x, z)
    arriving = {}

    row = lax.broadcasted_iota(jnp.int32, (SLOTS, tokens), 0)
    main = row < MAINS
    block = jnp.where(main, row // MAIN, (row - MAINS) // REST)
    slot = jnp.where(main, row % MAIN, MAIN + (row - MAINS) % REST).astype(F32)
    expert = x + block
    expert = jnp.where(expert >= EXPERTS, expert - EXPERTS, expert)
    earlier = (
        lax.broadcasted_iota(jnp.int32, (tokens, tokens), 0)
        < lax.broadcasted_iota(jnp.int32, (tokens, tokens), 1)
    ).astype(F32).astype(BF16)

    def layout(r_ref, p_ref):
        first, second = r_ref[0:1, :] == expert, r_ref[1:2, :] == expert
        chosen = jnp.where(first | second, 1.0, 0.0)
        before = nn(chosen.astype(BF16), earlier)
        taken = (before == slot) & (chosen > 0.5)
        weight = jnp.where(first, p_ref[0:1, :], 0.0) + jnp.where(second, p_ref[1:2, :], 0.0)
        return jnp.where(taken, 1.0, 0.0).astype(BF16), jnp.where(taken, weight, 0.0)

    def two(w):
        high = w.astype(BF16)
        return high, (w - high.astype(F32)).astype(BF16)

    def rest_out(tiles):
        a = lax.broadcasted_iota(jnp.int32, (MAINS, tiles * EXPERTS * REST), 0)
        b = lax.broadcasted_iota(jnp.int32, (MAINS, tiles * EXPERTS * REST), 1)
        source = (a % MAIN // REST) * (EXPERTS * REST) + (a // MAIN) * REST + a % REST
        return jnp.where(source == b, 1.0, 0.0).astype(BF16)

    moves = {size // LANE: rest_out(size // LANE) for _, size in all_cuts}

    def fold(rows, size):
        tiles = size // LANE
        stack = jnp.concatenate([rows[:, i * LANE:(i + 1) * LANE] for i in range(tiles)], axis=0)
        return nn(moves[tiles], stack).astype(BF16)

    def unfold(message, size):
        tiles, deep = size // LANE, EXPERTS * REST
        stack = tn(moves[tiles], message).astype(BF16)
        return jnp.concatenate([stack[i * deep:(i + 1) * deep] for i in range(tiles)], axis=1)

    def part(ref, c):
        at, size = parts[c]
        return ref[:, at:at + size]

    def scale_of(ref):
        total = jnp.zeros((tokens, 1), F32)
        for c in range(pieces):
            v = part(ref, c).astype(F32)
            total = total + jnp.sum(v * v, axis=-1, keepdims=True)
        return lax.rsqrt(total / width + EPS)

    def distribute(index, rows_of):
        for c, (at, size) in enumerate(parts):
            rows = rows_of(c).astype(BF16)
            low = fold(rows[MAINS:], size)
            tail = width + c * LANE
            packs[index, :, at:at + size] = rows[:MAINS]
            packs[index, :, tail:tail + LANE] = low
            tok[index, :MAIN, at:at + size] = rows[:MAIN]
            tok[index, :MAIN, tail:tail + LANE] = low[:MAIN]
        for k in range(1, EXPERTS):
            n = index * (EXPERTS - 1) + k - 1
            span = pl.ds(k * MAIN, MAIN)
            arriving["tok", index, k] = send(
                packs.at[index, span, :], tok.at[index, span, :],
                t_send.at[n], t_recv.at[n], place(s, at_x(k), z),
            )

    def normed(ref, pick):
        scale = scale_of(ref)
        return lambda c: nn(pick, (part(ref, c).astype(F32) * scale * part(gain_ref, c)).astype(BF16))

    pick_f, weight_f = layout(rf_ref, pf_ref)
    distribute(0, normed(x_ref, pick_f))
    pick_b, weight_b = layout(rb_ref, pb_ref)
    distribute(1, normed(act_ref, pick_b))
    high, low = two(weight_b)
    distribute(2, lambda c: nn(high, part(g_ref, c)) + nn(low, part(g_ref, c)))
    wf[...] = weight_f
    wb[...] = pick_b.astype(F32)
    arriving["x"] = send(x_ref, x_in, s_send.at[0], s_recv.at[0], ahead)
    arriving["wf"] = send(wf, wf_in, s_send.at[4], s_recv.at[4], ahead)
    arriving["act"] = send(act_ref, act_in, s_send.at[1], s_recv.at[1], behind)
    arriving["g"] = send(g_ref, g_in, s_send.at[2], s_recv.at[2], behind)
    arriving["gain"] = send(gain_ref, gain_in, s_send.at[3], s_recv.at[3], behind)
    arriving["wb"] = send(wb, wb_in, s_send.at[5], s_recv.at[5], behind)
    for copy in keep:
        copy.wait()

    def tokens_of(index):
        for k in range(1, EXPERTS):
            arriving["tok", index, k].wait_recv()
        for c, (at, size) in enumerate(parts):
            tail = width + c * LANE
            rest[index, :, at:at + size] = unfold(tok[index, :, tail:tail + LANE], size)

    def rows_of(index, c, which=parts):
        at, size = which[c]
        return [tok[index, :, at:at + size]], [rest[index, :, at:at + size]]

    def both_up(pair, c):
        one, other = (0, reach_a) if pair == 0 else (pair, reach_a + pair)
        at, size = parts[c]
        return jnp.concatenate([up[one, at:at + size, :], up[other, at:at + size, :]], axis=1)

    def both_down(pair, c):
        one, other = (0, reach_a) if pair == 0 else (pair, reach_a + pair)
        at, size = fine[c]
        return jnp.concatenate([down[one, :, at:at + size], down[other, :, at:at + size]], axis=0)

    def up_piece(c, pair):
        main_f, rest_f = rows_of(0, c)
        main_b, rest_b = rows_of(1, c)
        term = nn(jnp.concatenate(main_f + rest_f + main_b + rest_b, axis=0), both_up(pair, c))
        if c == 0:
            pre[pair] = term
        else:
            pre[pair] += term
        if c == pieces - 1:
            v = pre[pair, :SLOTS, :]
            hid[pair] = (v * jax.nn.sigmoid(v)).astype(BF16)

    def give_back(name, c, size, rows, src, dst, send_sem, recv_sem, section):
        src[c, :, :size] = rows[:MAINS]
        src[c, :, size:size + LANE] = fold(rows[MAINS:], size)
        for k in range(EXPERTS):
            span, lanes = pl.ds(k * MAIN, MAIN), pl.ds(0, size + LANE)
            arriving[name, c, k] = send(
                src.at[c, span, lanes], dst.at[c, span, lanes],
                send_sem.at[c, k], recv_sem.at[c, k], place(section, at_x(-k), z),
            )

    def down_back(c, pair):
        main_g, rest_g = rows_of(2, c, fine)
        term = nt(jnp.concatenate(main_g + rest_g, axis=0), both_down(pair, c))
        if c == 0:
            dh[pair] = term
        else:
            dh[pair] += term
        if c == fines - 1:
            v = pre[pair, SLOTS:, :]
            sig = jax.nn.sigmoid(v)
            dpre[pair] = (dh[pair] * sig * (1.0 + v * (1.0 - sig))).astype(BF16)

    def down_forward(c, pair):
        at, size = fine[c]
        term = nn(hid[pair], both_down(pair, c))
        if pair == 1 % pairs:
            out_acc[:, at:at + size] = term
        elif pair != 0:
            out_acc[:, at:at + size] += term
        else:
            rows = (out_acc[:, at:at + size] + term).astype(BF16)
            give_back("f", c, size, rows, ret_f, back_f, f_send, f_recv, nxt)

    def back_term(c, pair):
        at, size = parts[c]
        term = nt(dpre[pair], both_up(pair, c))
        if pair == 1 % pairs:
            dn_acc[:, at:at + size] = term
        else:
            dn_acc[:, at:at + size] += term

    waiting = []
    have_n = have_g = False
    for t in range(1, last + reach_a):
        if 3 <= t + 1 < last:
            start_own(t + 1)
        for r in range(1, reach_a + 1):
            c = t - r
            if 0 <= c < last:
                pass_round(c, r)
                waiting.append((c, r % reach_a))
        if t >= TOKEN_STEP:
            if not have_n:
                tokens_of(0)
                tokens_of(1)
                have_n = True
            for c, pair in waiting:
                if c < pieces:
                    up_piece(c, pair)
                    continue
                c = c - pieces
                if not have_g:
                    tokens_of(2)
                    have_g = True
                down_back(c, pair)
                if c < fines - 1 or pair != 0:
                    down_forward(c, pair)
                if c == fines - 1 and pair != 0:
                    for i in range(pieces):
                        back_term(i, pair)
            waiting = []

    order = [pieces - 1] + list(range(pieces - 1))
    for n, c in enumerate(order):
        at, size = parts[c]
        back_term(c, 0)
        give_back("b", c, size, dn_acc[:, at:at + size].astype(BF16), ret_b, back_b, b_send, b_recv, prv)
        if n == 0:
            down_forward(fines - 1, 0)

    for c, (at, size) in enumerate(parts):
        main_b, rest_b = rows_of(1, c)
        rows = jnp.concatenate(main_b + rest_b, axis=0).astype(F32)
        total = jnp.sum(rows * dn_acc[:, at:at + size], axis=0, keepdims=True)
        gpart[:, at:at + size] = total / part(gain_ref, c)
    gz[z] = gpart[...]
    for k in range(1, nz):
        send(gpart, gz.at[z], gz_send.at[k - 1], gz_recv.at[z], place(s, x, at_z(k)))

    def from_message(back, c, size):
        return jnp.concatenate([back[c, :, :size], unfold(back[c, :, size:size + LANE], size)], axis=0)

    for name in ("x", "wf", "act", "g", "gain", "wb"):
        arriving[name].wait_recv()
    scale = scale_of(act_in)
    high, low = two(wf_in[...])
    for c, (at, size) in enumerate(fine[:-1]):
        for k in range(EXPERTS):
            arriving["f", c, k].wait_recv()
        rows = from_message(back_f, c, size)
        act_out[:, at:at + size] = (x_in[:, at:at + size].astype(F32) + tn(high, rows) + tn(low, rows)).astype(BF16)

    for k in range(1, nz):
        frm = at_z(k)
        pltpu.make_async_remote_copy(
            src_ref=gpart, dst_ref=gz.at[frm], send_sem=gz_send.at[k - 1],
            recv_sem=gz_recv.at[frm], device_id=long_way, device_id_type=MESH,
        ).wait_recv()
    total = gz[0]
    for k in range(1, nz):
        total = total + gz[k]
    gx_own[...] = total
    gx[x] = total
    for k in range(1, EXPERTS):
        send(gx_own, gx.at[x], gx_send.at[k - 1], gx_recv.at[x], place(s, at_x(k), z))

    for c, (at, size) in list(enumerate(fine))[-1:]:
        for k in range(EXPERTS):
            arriving["f", c, k].wait_recv()
        rows = from_message(back_f, c, size)
        act_out[:, at:at + size] = (x_in[:, at:at + size].astype(F32) + tn(high, rows) + tn(low, rows)).astype(BF16)

    pick = wb_in[...].astype(BF16)
    dot = jnp.zeros((tokens, 1), F32)
    for c in order:
        at, size = parts[c]
        for k in range(EXPERTS):
            arriving["b", c, k].wait_recv()
        scaled = tn(pick, from_message(back_b, c, size)) * part(gain_in, c)
        qg[:, at:at + size] = scaled
        dot = dot + jnp.sum(scaled * (part(act_in, c).astype(F32) * scale), axis=-1, keepdims=True)
    mean = dot / width
    for c, (at, size) in enumerate(parts):
        xhat = part(act_in, c).astype(F32) * scale
        dx = part(g_in, c).astype(F32) + scale * (qg[:, at:at + size] - xhat * mean)
        grad_out[:, at:at + size] = dx.astype(BF16)

    for k in range(1, EXPERTS):
        frm = at_x(k)
        pltpu.make_async_remote_copy(
            src_ref=gx_own, dst_ref=gx.at[frm], send_sem=gx_send.at[k - 1],
            recv_sem=gx_recv.at[frm], device_id=long_way, device_id_type=MESH,
        ).wait_recv()
    total = gx[0]
    for k in range(1, EXPERTS):
        total = total + gx[k]
    gain_out[...] = total
    for copy in sent:
        copy.wait_send()


def body(sections, ranks, dp, x_fwd, gain, w_up, w_down, routes_f, probs_f, act_b, grad_b, routes_b, probs_b):
    zlo = ranks // EXPERTS
    nz = zlo * dp
    tokens, width = x_fwd.shape[1:]
    hidden = w_up.shape[-1]
    pairs = nz // 2
    pieces, fines = len(cuts(width)), len(cuts(width, FINE))
    last = pieces + fines
    span = width + pieces * LANE
    vmem, hbm = pl.BlockSpec(memory_space=pltpu.VMEM), pl.BlockSpec(memory_space=pl.ANY)
    dma = pltpu.SemaphoreType.DMA

    def bf16(*shape):
        return pltpu.VMEM(shape, BF16)

    def f32(*shape):
        return pltpu.VMEM(shape, F32)

    top = routes_f.shape[-1]
    routes = pltpu.VMEM((top, tokens), jnp.int32)
    scratch = [
        bf16(tokens, width), f32(1, width), routes, f32(top, tokens),
        bf16(tokens, width), bf16(tokens, width), routes, f32(top, tokens),
        bf16(nz, width, hidden), bf16(nz, hidden, width),
        bf16(3, MAINS, span), bf16(3, MAINS, span), bf16(3, SLOTS - MAINS, width),
        f32(pairs, 2 * SLOTS, 2 * hidden), bf16(pairs, SLOTS, 2 * hidden),
        f32(pairs, SLOTS, 2 * hidden), bf16(pairs, SLOTS, 2 * hidden),
        f32(SLOTS, width), f32(SLOTS, width),
    ]
    to_f, to_b = bf16(fines, MAINS, FINE + LANE), bf16(pieces, MAINS, PIECE + LANE)
    scratch += [to_f, to_b, to_f, to_b]
    scratch += [bf16(tokens, width)] * 3 + [f32(1, width)]
    scratch += [f32(SLOTS, tokens)] * 4 + [f32(tokens, width)]
    scratch += [f32(1, width), f32(nz, 1, width), f32(1, width), f32(EXPERTS, 1, width)]
    scratch += [
        dma((8,)), dma((2,)), dma((last, nz - 1)), dma((last, nz - 1)),
        dma((3 * (EXPERTS - 1),)), dma((3 * (EXPERTS - 1),)),
        dma((fines, EXPERTS)), dma((fines, EXPERTS)), dma((pieces, EXPERTS)), dma((pieces, EXPERTS)),
        dma((6,)), dma((6,)),
        dma((EXPERTS - 1,)), dma((EXPERTS,)), dma((nz - 1,)), dma((nz,)),
    ]
    act, grad, gain_grad = pl.pallas_call(
        functools.partial(relay, (sections, nz, zlo)),
        out_shape=(
            jax.ShapeDtypeStruct((tokens, width), BF16),
            jax.ShapeDtypeStruct((tokens, width), BF16),
            jax.ShapeDtypeStruct((1, width), F32),
        ),
        in_specs=[hbm] * 10,
        out_specs=(vmem, vmem, vmem),
        scratch_shapes=scratch,
        compiler_params=pltpu.CompilerParams(
            collective_id=0, has_side_effects=True, vmem_limit_bytes=56 * 2**20
        ),
    )(
        x_fwd[0], gain, w_up[0], w_down[0], routes_f[0].T, probs_f[0].T,
        act_b[0], grad_b[0], routes_b[0].T, probs_b[0].T,
    )
    return act[None], grad[None], gain_grad


def solution(mesh):
    sizes = mesh.shape
    rows, weights = P("section", ("expert", "dp"), None), P("section", None, ("expert", "dp"))
    return jax.shard_map(
        functools.partial(body, sizes["section"], sizes["expert"], sizes["dp"]),
        mesh=mesh,
        in_specs=(rows, P("section", None), weights) + (rows,) * 7,
        out_specs=(rows, rows, P("section", None)),
        check_vma=False,
    )
```

time: 197 us -> 179 us (0.909); the launches traced: 193 us -> 178 us
  Pallas kernels: 185 us -> 174 us
  local copies, waits for them, and re-layouts: 7.59 us -> 3.24 us
    pallas_call x1, Pallas kernels: 185 us -> 174 us  [body(): pl.pallas_call(functools.partial(relay, (sections, nz, zlo)), out_shape=(...]
    unnamed x17 -> x7, local copies, waits for them, and re-layouts: 7.21 us -> 3.24 us
where the time goes in v2:
time: 179 us; the launch traced here: 178 us
  Pallas kernels  174 us (97%)
  local copies, waits for them, and re-layouts  3.24 us (2%)
    pallas_call x1, Pallas kernels, body(): pl.pallas_call(functools.partial(relay, (sections, nz, zlo)), out_shape=(...  174 us

profile of v2, /device:TPU:56, one launch (start us, length us, event | category | flops | bytes accessed | tf_op | source)
XLA Modules:
  0.0 177.6 jit_solution(10319130719807272139)
XLA Ops:
  0.6 173.7 %shard_map.121 = (bf16[64,3584]{1,0:T(8,128)(2,1)}, bf16[64,3584]{1,0:T(8,128)(2,1)}, f32[1,3584]{1,0:T(1,128)}) custom-call(bf16[64,3584]{1,0:T(8,128)(2,1)} %bitcast.23, f32[1,3584]{1,0:T(1,128)} %gain_hbm.1, bf16[3584,128]{1,0:T(8,128)(2,1)} %bitcast.19, bf16[128,3584]{1,0:T(8,128)(2,1)} %bitcast.20, s32[2,64]{1,0:T(2,128)} %bitcast.26, ...), custom_call_target="tpu_custom_call" | custom-call | tf_op jit(solution)/shard_map/pallas_call | solution.py:458
  174.3 0.0 copy-start
  174.3 1.9 %copy.16 = bf16[1,64,3584]{2,1,0:T(8,128)(2,1)} copy(bf16[1,64,3584]{2,1,0:T(8,128)(2,1)} %bitcast.22) | data formatting | bytes 917504
  176.2 0.0 copy-done
  176.2 0.0 copy-start.1
  176.2 0.8 copy.17
  177.0 0.0 copy-done.1
  177.0 0.6 copy.18
Async XLA Ops:
  174.3 1.9 %copy-start = (bf16[64,3584]{1,0:T(8,128)(2,1)S(1)}, bf16[64,3584]{1,0:T(8,128)(2,1)}, u32[]{:S(2)}) copy-start(bf16[64,3584]{1,0:T(8,128)(2,1)} %get-tuple-element.7) | copy-start | bytes 1376260
  176.2 0.8 copy-start.1

commit v3 on v2

--- a/solution.py
+++ b/solution.py
@@ -15,8 +15,9 @@
 MAINS = EXPERTS * MAIN
 LANE = 128
 PIECE = LANE * MAIN // REST
-FINE = PIECE // 2
+FINE = PIECE // 4
 TOKEN_STEP = 4
+FARTHEST = (2, 1, 3, 0)
 MESH = pl.DeviceIdType.MESH
 F32 = jnp.float32
 BF16 = jnp.bfloat16
@@ -34,8 +35,17 @@
     return jnp.dot(a, b, preferred_element_type=F32)
 
 
-def cuts(width, piece=PIECE):
-    return [(at, min(piece, width - at)) for at in range(0, width, piece)]
+def cuts(width):
+    return [(at, min(PIECE, width - at)) for at in range(0, width, PIECE)]
+
+
+def fine_cuts(width):
+    found, at = [], 0
+    while at < width:
+        size = min(PIECE, width - at, max(FINE, (width - at) // 2 // FINE * FINE))
+        found.append((at, size))
+        at += size
+    return found
 
 
 def relay(
@@ -52,7 +62,7 @@
     tokens, width = x_ref.shape
     parts = cuts(width)
     pieces = len(parts)
-    fine = cuts(width, FINE)
+    fine = fine_cuts(width)
     fines = len(fine)
     all_cuts = parts + fine
     last = len(all_cuts)
@@ -201,7 +211,7 @@
             packs[index, :, tail:tail + LANE] = low
             tok[index, :MAIN, at:at + size] = rows[:MAIN]
             tok[index, :MAIN, tail:tail + LANE] = low[:MAIN]
-        for k in range(1, EXPERTS):
+        for k in FARTHEST[:-1]:
             n = index * (EXPERTS - 1) + k - 1
             span = pl.ds(k * MAIN, MAIN)
             arriving["tok", index, k] = send(
@@ -266,7 +276,7 @@
     def give_back(name, c, size, rows, src, dst, send_sem, recv_sem, section):
         src[c, :, :size] = rows[:MAINS]
         src[c, :, size:size + LANE] = fold(rows[MAINS:], size)
-        for k in range(EXPERTS):
+        for k in FARTHEST:
             span, lanes = pl.ds(k * MAIN, MAIN), pl.ds(0, size + LANE)
             arriving[name, c, k] = send(
                 src.at[c, span, lanes], dst.at[c, span, lanes],
@@ -336,12 +346,11 @@
             waiting = []
 
     order = [pieces - 1] + list(range(pieces - 1))
-    for n, c in enumerate(order):
+    for c in order:
         at, size = parts[c]
         back_term(c, 0)
         give_back("b", c, size, dn_acc[:, at:at + size].astype(BF16), ret_b, back_b, b_send, b_recv, prv)
-        if n == 0:
-            down_forward(fines - 1, 0)
+    down_forward(fines - 1, 0)
 
     for c, (at, size) in enumerate(parts):
         main_b, rest_b = rows_of(1, c)
@@ -378,12 +387,6 @@
     gx[x] = total
     for k in range(1, EXPERTS):
         send(gx_own, gx.at[x], gx_send.at[k - 1], gx_recv.at[x], place(s, at_x(k), z))
-
-    for c, (at, size) in list(enumerate(fine))[-1:]:
-        for k in range(EXPERTS):
-            arriving["f", c, k].wait_recv()
-        rows = from_message(back_f, c, size)
-        act_out[:, at:at + size] = (x_in[:, at:at + size].astype(F32) + tn(high, rows) + tn(low, rows)).astype(BF16)
 
     pick = wb_in[...].astype(BF16)
     dot = jnp.zeros((tokens, 1), F32)
@@ -400,6 +403,12 @@
         dx = part(g_in, c).astype(F32) + scale * (qg[:, at:at + size] - xhat * mean)
         grad_out[:, at:at + size] = dx.astype(BF16)
 
+    for c, (at, size) in list(enumerate(fine))[-1:]:
+        for k in range(EXPERTS):
+            arriving["f", c, k].wait_recv()
+        rows = from_message(back_f, c, size)
+        act_out[:, at:at + size] = (x_in[:, at:at + size].astype(F32) + tn(high, rows) + tn(low, rows)).astype(BF16)
+
     for k in range(1, EXPERTS):
         frm = at_x(k)
         pltpu.make_async_remote_copy(
@@ -420,7 +429,7 @@
     tokens, width = x_fwd.shape[1:]
     hidden = w_up.shape[-1]
     pairs = nz // 2
-    pieces, fines = len(cuts(width)), len(cuts(width, FINE))
+    pieces, fines = len(cuts(width)), len(fine_cuts(width))
     last = pieces + fines
     span = width + pieces * LANE
     vmem, hbm = pl.BlockSpec(memory_space=pltpu.VMEM), pl.BlockSpec(memory_space=pl.ANY)
@@ -443,7 +452,7 @@
         f32(pairs, SLOTS, 2 * hidden), bf16(pairs, SLOTS, 2 * hidden),
         f32(SLOTS, width), f32(SLOTS, width),
     ]
-    to_f, to_b = bf16(fines, MAINS, FINE + LANE), bf16(pieces, MAINS, PIECE + LANE)
+    to_f, to_b = bf16(fines, MAINS, PIECE + LANE), bf16(pieces, MAINS, PIECE + LANE)
     scratch += [to_f, to_b, to_f, to_b]
     scratch += [bf16(tokens, width)] * 3 + [f32(1, width)]
     scratch += [f32(SLOTS, tokens)] * 4 + [f32(tokens, width)]

time: 179 us -> 179 us (level)
  no operation moved by 1% of the time
where the time goes in v3:
time: 179 us; the launch traced here: 177 us
  Pallas kernels  173 us (97%)
  local copies, waits for them, and re-layouts  3.24 us (2%)
    pallas_call x1, Pallas kernels, body(): pl.pallas_call(functools.partial(relay, (sections, nz, zlo)), out_shape=(...  173 us

profile of v3, /device:TPU:56, one launch (start us, length us, event | category | flops | bytes accessed | tf_op | source)
XLA Modules:
  0.0 177.1 jit_solution(11538743293210303201)
XLA Ops:
  0.6 173.3 %shard_map.121 = (bf16[64,3584]{1,0:T(8,128)(2,1)}, bf16[64,3584]{1,0:T(8,128)(2,1)}, f32[1,3584]{1,0:T(1,128)}) custom-call(bf16[64,3584]{1,0:T(8,128)(2,1)} %bitcast.23, f32[1,3584]{1,0:T(1,128)} %gain_hbm.1, bf16[3584,128]{1,0:T(8,128)(2,1)} %bitcast.19, bf16[128,3584]{1,0:T(8,128)(2,1)} %bitcast.20, s32[2,64]{1,0:T(2,128)} %bitcast.26, ...), custom_call_target="tpu_custom_call" | custom-call | tf_op jit(solution)/shard_map/pallas_call | solution.py:467
  173.9 0.0 copy-start
  173.9 1.9 %copy.16 = bf16[1,64,3584]{2,1,0:T(8,128)(2,1)} copy(bf16[1,64,3584]{2,1,0:T(8,128)(2,1)} %bitcast.22) | data formatting | bytes 917504
  175.8 0.0 copy-done
  175.8 0.0 copy-start.1
  175.8 0.8 copy.17
  176.5 0.0 copy-done.1
  176.5 0.6 copy.18
Async XLA Ops:
  173.9 1.9 %copy-start = (bf16[64,3584]{1,0:T(8,128)(2,1)S(1)}, bf16[64,3584]{1,0:T(8,128)(2,1)}, u32[]{:S(2)}) copy-start(bf16[64,3584]{1,0:T(8,128)(2,1)} %get-tuple-element.7) | copy-start | bytes 1376260
  175.8 0.8 copy-start.1

commit v4 on v3

--- a/solution.py
+++ b/solution.py
@@ -314,7 +314,7 @@
         else:
             dn_acc[:, at:at + size] += term
 
-    waiting = []
+    waiting, ready = [], []
     have_n = have_g = False
     for t in range(1, last + reach_a):
         if 3 <= t + 1 < last:
@@ -341,9 +341,13 @@
                 if c < fines - 1 or pair != 0:
                     down_forward(c, pair)
                 if c == fines - 1 and pair != 0:
+                    ready.append(pair)
+            waiting = []
+            if t >= last + reach_a - 2:
+                for pair in ready:
                     for i in range(pieces):
                         back_term(i, pair)
-            waiting = []
+                ready = []
 
     order = [pieces - 1] + list(range(pieces - 1))
     for c in order:

time: 179 us -> 179 us (level)
  no operation moved by 1% of the time
where the time goes in v4:
time: 179 us; the launch traced here: 177 us
  Pallas kernels  173 us (97%)
  local copies, waits for them, and re-layouts  3.24 us (2%)
    pallas_call x1, Pallas kernels, body(): pl.pallas_call(functools.partial(relay, (sections, nz, zlo)), out_shape=(...  173 us

profile of v4, /device:TPU:56, one launch (start us, length us, event | category | flops | bytes accessed | tf_op | source)
XLA Modules:
  0.0 177.0 jit_solution(2993323518116932166)
XLA Ops:
  0.6 173.1 %shard_map.121 = (bf16[64,3584]{1,0:T(8,128)(2,1)}, bf16[64,3584]{1,0:T(8,128)(2,1)}, f32[1,3584]{1,0:T(1,128)}) custom-call(bf16[64,3584]{1,0:T(8,128)(2,1)} %bitcast.23, f32[1,3584]{1,0:T(1,128)} %gain_hbm.1, bf16[3584,128]{1,0:T(8,128)(2,1)} %bitcast.19, bf16[128,3584]{1,0:T(8,128)(2,1)} %bitcast.20, s32[2,64]{1,0:T(2,128)} %bitcast.26, ...), custom_call_target="tpu_custom_call" | custom-call | tf_op jit(solution)/shard_map/pallas_call | solution.py:471
  173.8 0.0 copy-start
  173.8 1.9 %copy.16 = bf16[1,64,3584]{2,1,0:T(8,128)(2,1)} copy(bf16[1,64,3584]{2,1,0:T(8,128)(2,1)} %bitcast.22) | data formatting | bytes 917504
  175.6 0.0 copy-done
  175.6 0.0 copy-start.1
  175.6 0.8 copy.17
  176.4 0.0 copy-done.1
  176.4 0.6 copy.18
Async XLA Ops:
  173.8 1.9 %copy-start = (bf16[64,3584]{1,0:T(8,128)(2,1)S(1)}, bf16[64,3584]{1,0:T(8,128)(2,1)}, u32[]{:S(2)}) copy-start(bf16[64,3584]{1,0:T(8,128)(2,1)} %get-tuple-element.7) | copy-start | bytes 1376260
  175.6 0.8 copy-start.1
